TPU v7x, 32 devices: a whole 2x2x4 slice. The times are simulated.
32 devices in a mesh: line: 4 (over y, x), cross: 8 (over z, core).
Axes of the slice: x: 2, y: 2, z: 4, core: 2. Of those that a mesh axis runs over, the one named last changes fastest.
Arguments:
- velocity: float32 [3, 512, 64, 256], P(None, 'line', 'cross'), may hold values from -6 to 6
Outputs:
- advection: float32 [3, 512, 64, 256], P(None, 'line', 'cross')
- x_derivative: float32 [3, 512, 64, 256], P(None, 'line', 'cross')
All inputs are finite; a program needn't handle non-finite values.
Results may differ from a plain program's by a relative error of at most 0.0001.
Values sent between devices are 32-bit elements; how exact they have to be, the bound alone decides.
A program may use at most 128 MiB of HBM per device.

v0:
```python
import jax
import jax.numpy as jnp
import numpy as np
from jax import lax
from jax.sharding import PartitionSpec as P

ALPHA = 1.0 / 3.0
COEF_A = 14.0 / 9.0
COEF_B = 1.0 / 9.0
FIRST = 45.0 / 60.0
SECOND = -9.0 / 60.0
THIRD = 1.0 / 60.0


def extended_2(block, sides, width):
    for axis, dim in sides:
        count = lax.axis_size(axis)
        forward = [(i, i + 1) for i in range(count - 1)]
        forward.append((count - 1, 0))
        backward = [(target, source) for source, target in forward]
        low = lax.ppermute(
            lax.slice_in_dim(block, block.shape[dim] - width, None, axis=dim), axis, forward
        )
        high = lax.ppermute(lax.slice_in_dim(block, 0, width, axis=dim), axis, backward)
        block = jnp.concatenate([low, block, high], axis=dim)
    return block


def passed_along(shard, axis, by):
    count = lax.axis_size(axis)
    return lax.ppermute(shard, axis, [(i, (i + by) % count) for i in range(count)])


def local_inverse(count):
    theta = np.ones(count + 1)
    for step in range(2, count + 1):
        theta[step] = theta[step - 1] - ALPHA * ALPHA * theta[step - 2]
    rows = np.arange(1, count + 1)[:, None]
    cols = np.arange(1, count + 1)[None, :]
    lower = np.minimum(rows, cols)
    upper = np.maximum(rows, cols)
    signs = np.power(-ALPHA, upper - lower)
    return signs * theta[lower - 1] * theta[count - upper] / theta[count]


def explicit_x(extended, count):
    near = extended[:, 3 : 3 + count] - extended[:, 1 : 1 + count]
    far = extended[:, 4 : 4 + count] - extended[:, 0:count]
    return 0.5 * COEF_A * near + 0.25 * COEF_B * far


def apply_rows(table, values):
    return jnp.einsum("ij,cjyz->ciyz", table, values, precision=lax.Precision.HIGHEST)


def explicit_z(field):
    total = FIRST * (jnp.roll(field, -1, 3) - jnp.roll(field, 1, 3))
    total = total + SECOND * (jnp.roll(field, -2, 3) - jnp.roll(field, 2, 3))
    return total + THIRD * (jnp.roll(field, -3, 3) - jnp.roll(field, 3, 3))


def stencil_y(padded, count):
    total = FIRST * (padded[:, :, 4 : 4 + count] - padded[:, :, 2 : 2 + count])
    total = total + SECOND * (padded[:, :, 5 : 5 + count] - padded[:, :, 1 : 1 + count])
    return total + THIRD * (padded[:, :, 6 : 6 + count] - padded[:, :, 0:count])


def on_device(velocity):
    seg_len = velocity.shape[1]
    tile_len = velocity.shape[2]
    extended = extended_2(velocity, (("line", 1),), 2)
    forcing = explicit_x(extended, seg_len)
    inverse = local_inverse(seg_len)
    table = jnp.asarray(inverse, jnp.float32)
    partial_sol = apply_rows(table, forcing)
    ends = jnp.stack([partial_sol[:, 0], partial_sol[:, -1]], axis=1)
    beside_all = extended_2(ends, (("line", 1),), 1)
    corner = float(inverse[0, 0])
    denom = 1.0 - ALPHA * ALPHA * corner * corner
    left_value = (beside_all[:, 0] - ALPHA * corner * partial_sol[:, 0]) / denom
    right_value = (beside_all[:, 3] - ALPHA * corner * partial_sol[:, -1]) / denom
    first_col = table[:, 0][None, :, None, None]
    last_col = table[:, -1][None, :, None, None]
    along_x = partial_sol - ALPHA * (
        left_value[:, None] * first_col + right_value[:, None] * last_col
    )
    zero_pad = jnp.pad(velocity, ((0, 0), (0, 0), (3, 3), (0, 0)))
    along_y = stencil_y(zero_pad, tile_len)
    head0 = velocity[:, :, 0]
    head1 = velocity[:, :, 1]
    head2 = velocity[:, :, 2]
    for_before = jnp.stack(
        [
            THIRD * head0,
            SECOND * head0 + THIRD * head1,
            FIRST * head0 + SECOND * head1 + THIRD * head2,
        ],
        axis=2,
    )
    tail0 = velocity[:, :, -1]
    tail1 = velocity[:, :, -2]
    tail2 = velocity[:, :, -3]
    for_after = -jnp.stack(
        [
            FIRST * tail0 + SECOND * tail1 + THIRD * tail2,
            SECOND * tail0 + THIRD * tail1,
            THIRD * tail0,
        ],
        axis=2,
    )
    from_after = passed_along(for_before, "cross", -1)
    from_before = passed_along(for_after, "cross", 1)
    along_y = along_y.at[:, :, tile_len - 3 :].add(from_after)
    along_y = along_y.at[:, :, 0:3].add(from_before)
    along_z = explicit_z(velocity)
    speed_u = velocity[0:1]
    speed_v = velocity[1:2]
    speed_w = velocity[2:3]
    advection = -(speed_u * along_x + speed_v * along_y + speed_w * along_z)
    return (advection, along_x)


def solution(mesh):
    in_specs = (P(None, "line", "cross", None),)
    out_specs = (P(None, "line", "cross", None), P(None, "line", "cross", None))
    return jax.shard_map(
        on_device, mesh=mesh, in_specs=in_specs, out_specs=out_specs, check_vma=False
    )
```

profile of v0, /device:TPU:0, one launch (start us, length us, event | category | flops | bytes accessed | tf_op | source)
XLA Modules:
  0.0 69.3 jit_solution(13641333226833702118)
XLA Ops:
  0.6 0.8 %fusion.29 = (f32[3,2,8,256]{3,2,1,0:T(8,128)S(1)}, f32[3,2,8,256]{3,2,1,0:T(8,128)S(1)}) fusion(f32[3,128,8,256]{3,2,1,0:T(8,128)} %param.6), kind=kLoop, calls=%fused_computation.60 | loop fusion | bytes 196608 | tf_op jit(solution)/shard_map/slice | solution.py:24
  1.5 3.9 %collective-permute-start = (f32[3,2,8,256]{3,2,1,0:T(8,128)S(1)}, f32[3,2,8,256]{3,2,1,0:T(8,128)S(1)}, u32[]{:S(2)}, u32[]{:S(2)}) collective-permute-start(f32[3,2,8,256]{3,2,1,0:T(8,128)S(1)} %get-tuple-element.34), channel_id=1, source_target_pairs={{8,0},{16,8},{24,16},{0,24},{9,1},{17,9},{25,17},{1,25},{10,2},{18... | collective-permute-start | bytes 147464 | tf_op jit(solution)/shard_map/ppermute | solution.py:24
  5.4 2.9 %copy.7 = f32[3,128,8,256]{3,1,2,0:T(8,128)S(1)} copy(f32[3,128,8,256]{3,2,1,0:T(8,128)} %param.6) | data formatting | bytes 6291456 | tf_op args[0]
  8.3 0.3 fusion.26
  8.7 2.8 %collective-permute-start.4 = (f32[3,128,3,256]{3,1,2,0:T(8,128)S(1)}, f32[3,128,3,256]{3,1,2,0:T(8,128)S(1)}, u32[]{:S(2)}, u32[]{:S(2)}) collective-permute-start(f32[3,128,3,256]{3,1,2,0:T(8,128)S(1)} %pad_maximum_fusion), channel_id=1, source_target_pairs={{0,7},{1,0},{2,1},{3,2},{4,3},{5,4},{6,5},{7,6},{8,15},{9,8},{10,9... | collective-permute-start | bytes 3538952 | tf_op jit(solution)/shard_map/ppermute | solution.py:31
  11.7 1.7 %fusion.34 = (f32[3,128,8,1]{3,1,2,0:T(8,128)S(1)}, f32[3,128,8,1]{3,1,2,0:T(8,128)}) fusion(f32[3,128,8,256]{3,1,2,0:T(8,128)S(1)} %copy.7), kind=kLoop, calls=%fused_computation.65 | loop fusion | bytes 49152 | tf_op jit(solution)/shard_map/jit(_roll_static)/slice | solution.py:57
  13.4 2.3 %fusion.30 = (f32[3,128,8,3]{3,1,2,0:T(8,128)}, f32[3,128,8,3]{3,1,2,0:T(8,128)}) fusion(f32[3,128,8,256]{3,1,2,0:T(8,128)S(1)} %copy.7), kind=kLoop, calls=%fused_computation.61 | loop fusion | bytes 147456 | tf_op jit(solution)/shard_map/jit(_roll_static)/slice | solution.py:59
  15.8 2.3 %fusion.32 = (f32[3,128,8,2]{3,1,2,0:T(8,128)}, f32[3,128,8,2]{3,1,2,0:T(8,128)}) fusion(f32[3,128,8,256]{3,1,2,0:T(8,128)S(1)} %copy.7), kind=kLoop, calls=%fused_computation.63 | loop fusion | bytes 98304 | tf_op jit(solution)/shard_map/jit(_roll_static)/slice | solution.py:58
  18.0 3.9 %fusion.31 = (f32[3,128,8,253]{3,1,2,0:T(8,128)}, f32[3,128,8,253]{3,1,2,0:T(8,128)}) fusion(f32[3,128,8,256]{3,1,2,0:T(8,128)S(1)} %copy.7), kind=kLoop, calls=%fused_computation.62 | loop fusion | bytes 12435456 | tf_op jit(solution)/shard_map/jit(_roll_static)/slice | solution.py:59
  21.9 3.9 %fusion.35 = (f32[3,128,8,255]{3,1,2,0:T(8,128)}, f32[3,128,8,255]{3,1,2,0:T(8,128)}) fusion(f32[3,128,8,256]{3,1,2,0:T(8,128)S(1)} %copy.7), kind=kLoop, calls=%fused_computation.66 | loop fusion | bytes 12533760 | tf_op jit(solution)/shard_map/jit(_roll_static)/slice | solution.py:57
  25.8 3.8 %fusion.33 = (f32[3,128,8,254]{3,1,2,0:T(8,128)}, f32[3,128,8,254]{3,1,2,0:T(8,128)}) fusion(f32[3,128,8,256]{3,1,2,0:T(8,128)S(1)} %copy.7), kind=kLoop, calls=%fused_computation.64 | loop fusion | bytes 12484608 | tf_op jit(solution)/shard_map/jit(_roll_static)/slice | solution.py:58
  29.9 0.5 constant_dynamic-update-slice_fusion.1
  30.5 0.5 fusion.9
  31.0 0.3 copy-done.3
  31.3 4.0 %fusion.21 = f32[3,128,8,256]{3,1,2,0:T(8,128)S(1)} fusion(f32[128,128,1,1]{1,0,3,2:T(8,128)S(1)} %copy-done.3, f32[3,128,8,256]{3,2,1,0:T(8,128)S(1)} %fusion.9), kind=kOutput, calls=%fused_computation.33 | convolution fusion | flops 1207959552 | bytes 6356992 | tf_op jit(solution)/shard_map/ij,cjyz->ciyz/dot_general | solution.py:53
  35.3 1.7 %collective-permute-start.2 = (f32[3,1,8,256]{3,1,2,0:T(1,128)S(1)}, f32[3,1,8,256]{3,1,2,0:T(1,128)S(1)}, u32[]{:S(2)}, u32[]{:S(2)}) collective-permute-start(f32[3,1,8,256]{3,1,2,0:T(1,128)S(1)} %get-tuple-element.32), channel_id=1, source_target_pairs={{0,8},{8,16},{16,24},{24,0},{1,9},{9,17},{17,25},{25,1},{2,10},{10... | collective-permute-start | bytes 73736 | tf_op jit(solution)/shard_map/ppermute | solution.py:21
  37.0 1.2 %collective-permute-start.3 = (f32[3,1,8,256]{3,1,2,0:T(1,128)S(1)}, f32[3,1,8,256]{3,1,2,0:T(1,128)S(1)}, u32[]{:S(2)}, u32[]{:S(2)}) collective-permute-start(f32[3,1,8,256]{3,1,2,0:T(1,128)S(1)} %get-tuple-element.33), channel_id=1, source_target_pairs={{8,0},{16,8},{24,16},{0,24},{9,1},{17,9},{25,17},{1,25},{10,2},{18... | collective-permute-start | bytes 73736 | tf_op jit(solution)/shard_map/ppermute | solution.py:24
  38.3 1.5 %fusion.3 = f32[3,128,8,256]{3,1,2,0:T(8,128)S(1)} fusion(f32[3,128,8,256]{3,1,2,0:T(8,128)S(1)} %copy.7), kind=kLoop, calls=%fused_computation.9 | loop fusion | flops 6291456 | bytes 6291456 | tf_op jit(solution)/shard_map/add | solution.py:65
  39.8 1.3 %copy.4 = f32[128,8,256]{2,0,1:T(8,128)} copy(f32[128,8,256]{2,1,0:T(8,128)S(1)} %get-tuple-element.38) | data formatting | bytes 2097152 | tf_op jit(solution)/shard_map/mul | solution.py:119
  41.2 1.3 %copy.6 = f32[128,8,256]{2,0,1:T(8,128)} copy(f32[128,8,256]{2,1,0:T(8,128)S(1)} %get-tuple-element.39) | data formatting | bytes 2097152 | tf_op jit(solution)/shard_map/mul | solution.py:119
  42.4 1.3 %copy.14 = f32[128,8,256]{2,0,1:T(8,128)} copy(f32[128,8,256]{2,1,0:T(8,128)S(1)} %get-tuple-element.40) | data formatting | bytes 2097152 | tf_op jit(solution)/shard_map/mul | solution.py:119
  44.5 15.7 %fusion.16 = (f32[3,128,8,256]{3,1,2,0:T(8,128)}, f32[3,128,8,256]{3,1,2,0:T(8,128)}) fusion(f32[3,128,8,1]{3,1,2,0:T(8,128)} %get-tuple-element.56, f32[3,128,8,255]{3,1,2,0:T(8,128)} %get-tuple-element.58, f32[3,128,8,255]{3,1,2,0:T(8,128)} %get-tuple-element.57, f32[3,128,8,1]{3,1,2,0:T(8,128)S(1)} %get-tuple-element.55, ...), kind=kLoop, calls=%fused_computation.25 | loop fusion | flops 19660800 | bytes 34653184 | tf_op jit(solution)/shard_map/neg | solution.py:119
  60.3 5.5 %copy.27 = f32[3,128,8,256]{3,2,1,0:T(8,128)} copy(f32[3,128,8,256]{3,1,2,0:T(8,128)} %get-tuple-element.28) | data formatting | bytes 6291456
  65.8 3.5 %copy.28 = f32[3,128,8,256]{3,2,1,0:T(8,128)} copy(f32[3,128,8,256]{3,1,2,0:T(8,128)S(1)} %copy-done.2) | data formatting | bytes 6291456
  (29 shorter events, 1.2 us)
Async XLA Ops:
  1.5 29.0 %collective-permute-start = (f32[3,2,8,256]{3,2,1,0:T(8,128)S(1)}, f32[3,2,8,256]{3,2,1,0:T(8,128)S(1)}, u32[]{:S(2)}, u32[]{:S(2)}) collective-permute-start(f32[3,2,8,256]{3,2,1,0:T(8,128)S(1)} %get-tuple-element.34), channel_id=1, source_target_pairs={{8,0},{16,8},{24,16},{0,24},{9,1},{17,9},{25,17},{1,25},{10,2},{18... | collective-permute-start | bytes 147464 | tf_op jit(solution)/shard_map/ppermute | solution.py:24
  5.4 24.4 %collective-permute-start.1 = (f32[3,2,8,256]{3,2,1,0:T(8,128)S(1)}, f32[3,2,8,256]{3,2,1,0:T(8,128)S(1)}, u32[]{:S(2)}, u32[]{:S(2)}) collective-permute-start(f32[3,2,8,256]{3,2,1,0:T(8,128)S(1)} %get-tuple-element.35), channel_id=1, source_target_pairs={{0,8},{8,16},{16,24},{24,0},{1,9},{9,17},{17,25},{25,1},{2,10},{10... | collective-permute-start | bytes 147464 | tf_op jit(solution)/shard_map/ppermute | solution.py:21
  8.7 35.2 %collective-permute-start.4 = (f32[3,128,3,256]{3,1,2,0:T(8,128)S(1)}, f32[3,128,3,256]{3,1,2,0:T(8,128)S(1)}, u32[]{:S(2)}, u32[]{:S(2)}) collective-permute-start(f32[3,128,3,256]{3,1,2,0:T(8,128)S(1)} %pad_maximum_fusion), channel_id=1, source_target_pairs={{0,7},{1,0},{2,1},{3,2},{4,3},{5,4},{6,5},{7,6},{8,15},{9,8},{10,9... | collective-permute-start | bytes 3538952 | tf_op jit(solution)/shard_map/ppermute | solution.py:31
  11.6 32.6 %collective-permute-start.5 = (f32[3,128,3,256]{3,1,2,0:T(8,128)S(1)}, f32[3,128,3,256]{3,1,2,0:T(8,128)S(1)}, u32[]{:S(2)}, u32[]{:S(2)}) collective-permute-start(f32[3,128,3,256]{3,1,2,0:T(8,128)S(1)} %maximum_negate_fusion), channel_id=1, source_target_pairs={{0,1},{1,2},{2,3},{3,4},{4,5},{5,6},{6,7},{7,0},{8,9},{9,10},{10,1... | collective-permute-start | bytes 3538952 | tf_op jit(solution)/shard_map/ppermute | solution.py:31
  25.8 3.8 %copy-start = (f32[3,128,8,256]{3,2,1,0:T(8,128)S(1)}, f32[3,128,8,256]{3,2,1,0:T(8,128)}, u32[]{:S(2)}) copy-start(f32[3,128,8,256]{3,2,1,0:T(8,128)} %param.6) | copy-start | bytes 9437188
  30.4 0.8 %copy-start.3 = (f32[128,128,1,1]{1,0,3,2:T(8,128)S(1)}, f32[128,128,1,1]{1,0,3,2:T(8,128)}, u32[]{:S(2)}) copy-start(f32[128,128,1,1]{1,0,3,2:T(8,128)} %constant.88) | copy-start | bytes 196612
  35.3 8.5 %copy-start.1 = (f32[3,128,8,256]{3,1,2,0:T(8,128)}, f32[3,128,8,256]{3,1,2,0:T(8,128)S(1)}, u32[]{:S(2)}) copy-start(f32[3,128,8,256]{3,1,2,0:T(8,128)S(1)} %fusion.21) | copy-start | bytes 9437188
  35.3 8.4 %collective-permute-start.2 = (f32[3,1,8,256]{3,1,2,0:T(1,128)S(1)}, f32[3,1,8,256]{3,1,2,0:T(1,128)S(1)}, u32[]{:S(2)}, u32[]{:S(2)}) collective-permute-start(f32[3,1,8,256]{3,1,2,0:T(1,128)S(1)} %get-tuple-element.32), channel_id=1, source_target_pairs={{0,8},{8,16},{16,24},{24,0},{1,9},{9,17},{17,25},{25,1},{2,10},{10... | collective-permute-start | bytes 73736 | tf_op jit(solution)/shard_map/ppermute | solution.py:21
  37.0 6.7 %collective-permute-start.3 = (f32[3,1,8,256]{3,1,2,0:T(1,128)S(1)}, f32[3,1,8,256]{3,1,2,0:T(1,128)S(1)}, u32[]{:S(2)}, u32[]{:S(2)}) collective-permute-start(f32[3,1,8,256]{3,1,2,0:T(1,128)S(1)} %get-tuple-element.33), channel_id=1, source_target_pairs={{8,0},{16,8},{24,16},{0,24},{9,1},{17,9},{25,17},{1,25},{10,2},{18... | collective-permute-start | bytes 73736 | tf_op jit(solution)/shard_map/ppermute | solution.py:24
  43.9 0.7 copy-start.4
  43.9 0.7 copy-start.5
  60.3 5.5 %copy-start.2 = (f32[3,128,8,256]{3,1,2,0:T(8,128)S(1)}, f32[3,128,8,256]{3,1,2,0:T(8,128)}, u32[]{:S(2)}) copy-start(f32[3,128,8,256]{3,1,2,0:T(8,128)} %get-tuple-element.29) | copy-start | bytes 9437188
where the time goes:
time: 69.6 us; the launch traced here: 69.3 us
  local copies, waits for them, and re-layouts  35.7 us (51%)
  other arithmetic  19 us (27%)
  starting transfers between devices  9.78 us (14%)
  matrix products  3.96 us (6%)
  between operations  0.84 us (1%)
    neg x1, other arithmetic, on_device(): advection = -(speed_u * along_x + speed_v * along_y + speed_w * along_z)  15.7 us
    unnamed x18, local copies, waits for them, and re-layouts  12.8 us
    slice x2, local copies, waits for them, and re-layouts, explicit_z(): return total + THIRD * (jnp.roll(field, -3, 3) - jnp.roll(field, 3, 3))  6.21 us
    slice x2, local copies, waits for them, and re-layouts, explicit_z(): total = total + SECOND * (jnp.roll(field, -2, 3) - jnp.roll(field, 2, 3))  6.06 us
    slice x2, local copies, waits for them, and re-layouts, explicit_z(): total = FIRST * (jnp.roll(field, -1, 3) - jnp.roll(field, 1, 3))  5.66 us
    ppermute x2, starting transfers between devices, extended_2(): lax.ppermute(lax.slice_in_dim(block, 0, width, axis=dim), axis, backward)  5.17 us
    mul x4, local copies, waits for them, and re-layouts, on_device(): advection = -(speed_u * along_x + speed_v * along_y + speed_w * along_z)  4.11 us
    dot_general x1, matrix products, apply_rows(): jnp.einsum('ij,cjyz->ciyz', table, values, precision=lax.Precision.HIGHEST)  3.96 us
  transfers between devices with their start and end apart: 6, of which 0 were waited for; matrix products, arithmetic and copies ran while one was open for 47% of the time, Pallas kernels for 0%

commit v1 on v0

v1 whole, which is shorter than its diff:
```python
import functools
import math

import jax
import jax.numpy as jnp
from jax import lax
from jax.experimental import pallas as pl
from jax.experimental.pallas import tpu as pltpu
from jax.sharding import PartitionSpec as P

MESH = pl.DeviceIdType.MESH
ALPHA = 1.0 / 3.0
NEAR = 7.0 / 9.0
FAR = 1.0 / 36.0
ROOT = (math.sqrt(1.0 - 4.0 * ALPHA * ALPHA) - 1.0) / (2.0 * ALPHA)
SCALE = 1.0 + ROOT * ROOT
STENCIL = (45.0 / 60.0, -9.0 / 60.0, 1.0 / 60.0)
WIDTH = 3
CHUNKS = 8
COMPS = 3


def kernel(
    lines,
    tiles,
    vel,
    adv,
    gx,
    vx,
    halo,
    ends,
    beside,
    power,
    in_sem,
    y_send,
    y_recv,
    x_send,
    x_recv,
    e_send,
    e_recv,
):
    seg = vel.shape[1]
    rows = vel.shape[2]
    chunk = seg // CHUNKS
    line = lax.axis_index("line")
    tile = lax.axis_index("cross")
    ahead = (lax.rem(line + 1, lines), tile)
    behind = (lax.rem(line + lines - 1, lines), tile)
    above = (line, lax.rem(tile + 1, tiles))
    below = (line, lax.rem(tile + tiles - 1, tiles))

    local = pltpu.make_async_copy(vel, vx.at[:, 2 : 2 + seg], in_sem)
    local.start()

    barrier = pltpu.get_barrier_semaphore()
    for device in (above, below, ahead, behind):
        pl.semaphore_signal(barrier, inc=1, device_id=device, device_id_type=MESH)
    pl.semaphore_wait(barrier, 4)

    def remote(src, dst, send, recv, device):
        return pltpu.make_async_remote_copy(
            src_ref=src,
            dst_ref=dst,
            send_sem=send,
            recv_sem=recv,
            device_id=device,
            device_id_type=MESH,
        )

    x_copies = [
        remote(vel.at[:, seg - 2 : seg], vx.at[:, 0:2], x_send.at[0], x_recv.at[0], ahead),
        remote(vel.at[:, 0:2], vx.at[:, seg + 2 : seg + 4], x_send.at[1], x_recv.at[1], behind),
    ]
    for copy in x_copies:
        copy.start()

    y_copies = []
    for part in range(CHUNKS):
        planes = slice(part * chunk, (part + 1) * chunk)
        head = slice(0, WIDTH)
        tail = slice(rows - WIDTH, rows)
        pair = (
            remote(
                vel.at[:, planes, tail],
                halo.at[:, planes, tail],
                y_send.at[0, part],
                y_recv.at[0, part],
                above,
            ),
            remote(
                vel.at[:, planes, head],
                halo.at[:, planes, head],
                y_send.at[1, part],
                y_recv.at[1, part],
                below,
            ),
        )
        for copy in pair:
            copy.start()
        y_copies.append(pair)

    def fill(i, value):
        power[i] = value
        return value * ROOT

    lax.fori_loop(0, seg, fill, jnp.float32(ROOT))

    local.wait()
    for copy in x_copies:
        copy.wait()

    zero = jnp.zeros((COMPS,) + vel.shape[2:], jnp.float32)

    def forward(i, before):
        near = vx[:, i + 3] - vx[:, i + 1]
        far = vx[:, i + 4] - vx[:, i]
        now = (NEAR * near + FAR * far) + ROOT * before
        gx[:, i] = now
        return now

    ends[0] = lax.fori_loop(0, seg, forward, zero, unroll=4)

    def backward(k, after):
        i = seg - 1 - k
        now = SCALE * gx[:, i] + ROOT * after
        gx[:, i] = now
        return now

    ends[1] = lax.fori_loop(0, seg, backward, zero, unroll=4)

    e_copies = [
        remote(ends.at[0], beside.at[0], e_send.at[0], e_recv.at[0], ahead),
        remote(ends.at[1], beside.at[1], e_send.at[1], e_recv.at[1], behind),
    ]
    for copy in e_copies:
        copy.start()

    depth = vel.shape[3]

    def along_z(i, carry):
        w = vx[2, i + 2]
        for c in range(COMPS):
            field = vx[c, i + 2]
            total = None
            for k, weight in enumerate(STENCIL, 1):
                diff = pltpu.roll(field, depth - k, 1) - pltpu.roll(field, k, 1)
                total = weight * diff if total is None else total + weight * diff
            adv[c, i] = w * total
        return carry

    lax.fori_loop(0, seg, along_z, 0, unroll=2)

    for copy in e_copies:
        copy.wait()

    gain = SCALE / (1.0 - ROOT * ROOT)
    left = gain * beside[0]
    right = beside[1] + (gain * ROOT) * ends[0] - (gain * ROOT ** (seg + 1)) * beside[0]

    def along_x(i, carry):
        u = vx[0, i + 2]
        for c in range(COMPS):
            value = gx[c, i] + (power[i] * left[c] + power[seg - 1 - i] * right[c])
            gx[c, i] = value
            adv[c, i] = adv[c, i] + u * value
        return carry

    lax.fori_loop(0, seg, along_x, 0, unroll=2)

    row = lax.broadcasted_iota(jnp.int32, vel.shape[2:], 0)

    def along_y(i, carry):
        v = vx[1, i + 2]
        for c in range(COMPS):
            field = vx[c, i + 2]
            other = halo[c, i]
            total = None
            for k, weight in enumerate(STENCIL, 1):
                up = pltpu.roll(jnp.where(row < k, other, field), rows - k, 0)
                down = pltpu.roll(jnp.where(row >= rows - k, other, field), k, 0)
                diff = up - down
                total = weight * diff if total is None else total + weight * diff
            adv[c, i] = -(adv[c, i] + v * total)
        return carry

    for part in range(CHUNKS):
        for copy in y_copies[part]:
            copy.wait_recv()
        lax.fori_loop(part * chunk, (part + 1) * chunk, along_y, 0, unroll=2)
    for pair in y_copies:
        for copy in pair:
            copy.wait_send()


def on_device(lines, tiles, velocity):
    comps, seg, rows, depth = velocity.shape
    plane = (comps, rows, depth)
    shape = jax.ShapeDtypeStruct(velocity.shape, jnp.float32)
    adv, gx = pl.pallas_call(
        functools.partial(kernel, lines, tiles),
        out_shape=(shape, shape),
        in_specs=[pl.BlockSpec(memory_space=pl.ANY)],
        out_specs=(
            pl.BlockSpec(memory_space=pltpu.VMEM),
            pl.BlockSpec(memory_space=pltpu.VMEM),
        ),
        scratch_shapes=[
            pltpu.VMEM((comps, seg + 4, rows, depth), jnp.float32),
            pltpu.VMEM(velocity.shape, jnp.float32),
            pltpu.VMEM((2,) + plane, jnp.float32),
            pltpu.VMEM((2,) + plane, jnp.float32),
            pltpu.SMEM((seg,), jnp.float32),
            pltpu.SemaphoreType.DMA,
            pltpu.SemaphoreType.DMA((2, CHUNKS)),
            pltpu.SemaphoreType.DMA((2, CHUNKS)),
            pltpu.SemaphoreType.DMA((2,)),
            pltpu.SemaphoreType.DMA((2,)),
            pltpu.SemaphoreType.DMA((2,)),
            pltpu.SemaphoreType.DMA((2,)),
        ],
        compiler_params=pltpu.CompilerParams(
            collective_id=0, has_side_effects=True, vmem_limit_bytes=40 * 1024 * 1024
        ),
    )(velocity)
    return adv, gx


def solution(mesh):
    spec = P(None, "line", "cross", None)
    return jax.shard_map(
        functools.partial(on_device, mesh.shape["line"], mesh.shape["cross"]),
        mesh=mesh,
        in_specs=(spec,),
        out_specs=(spec, spec),
        check_vma=False,
    )
```

time: 69.6 us -> 39.1 us (0.56)
  Pallas kernels: 0 us -> 33.1 us
  local copies, waits for them, and re-layouts: 35.7 us -> 5.21 us
  other arithmetic: 19 us -> 0 us
  starting transfers between devices: 9.78 us -> 0 us
  matrix products: 3.96 us -> 0 us
    pallas_call x0 -> x1, Pallas kernels: none -> 33.1 us  [on_device(): pl.pallas_call(functools.partial(kernel, lines, tiles), out_shape=(shape,...]
    slice x8 -> x0, local copies, waits for them, and re-layouts: 18.8 us -> none  [the longest x2 6.21 us: explicit_z(): return total + THIRD * (jnp.roll(field, -3, 3) - jnp.roll(field, 3, 3))]
    neg x2 -> x0, other arithmetic: 15.8 us -> none  [the longest x1 15.7 us: on_device(): advection = -(speed_u * along_x + speed_v * along_y + speed_w * along_z)]
    ppermute x6 -> x0, starting transfers between devices: 9.78 us -> none  [the longest x2 5.17 us: extended_2(): lax.ppermute(lax.slice_in_dim(block, 0, width, axis=dim), axis, backward)]
    unnamed x18 -> x4, local copies, waits for them, and re-layouts: 12.8 us -> 5.21 us
    mul x4 -> x0, local copies, waits for them, and re-layouts: 4.11 us -> none  [on_device(): advection = -(speed_u * along_x + speed_v * along_y + speed_w * along_z)]
    dot_general x1 -> x0, matrix products: 3.96 us -> none  [apply_rows(): jnp.einsum('ij,cjyz->ciyz', table, values, precision=lax.Precision.HIGHEST)]
    add x3 -> x0, other arithmetic: 2.39 us -> none  [the longest x1 1.55 us: stencil_y(): return total + THIRD * (padded[:, :, 6:6 + count] - padded[:, :, 0:count])]
  transfers between devices with their start and end apart: 6 -> 0, of which waited for: 0 -> 0; matrix products, arithmetic and copies ran while one was open for 47% -> 0% of each run, Pallas kernels for 0% -> 0%
where the time goes in v1:
time: 39.1 us; the launch traced here: 38.9 us
  Pallas kernels  33.1 us (85%)
  local copies, waits for them, and re-layouts  5.21 us (13%)
  between operations  0.65 us (2%)
    pallas_call x1, Pallas kernels, on_device(): pl.pallas_call(functools.partial(kernel, lines, tiles), out_shape=(shape,...  33.1 us
    unnamed x4, local copies, waits for them, and re-layouts  5.21 us

profile of v1, /device:TPU:0, one launch (start us, length us, event | category | flops | bytes accessed | tf_op | source)
XLA Modules:
  0.0 38.9 jit_solution(9780596194786084415)
XLA Ops:
  0.6 0.0 copy-start
  0.6 1.9 %copy-done = f32[3,128,8,256]{3,2,1,0:T(8,128)S(1)} copy-done((f32[3,128,8,256]{3,2,1,0:T(8,128)S(1)}, f32[3,128,8,256]{3,2,1,0:T(8,128)}, u32[]{:S(2)}) %copy-start) | copy-done | bytes 3145752
  2.5 33.1 %shard_map.30 = (f32[3,128,8,256]{3,2,1,0:T(8,128)S(1)}, f32[3,128,8,256]{3,2,1,0:T(8,128)S(1)}) custom-call(f32[3,128,8,256]{3,2,1,0:T(8,128)S(1)} %copy-done), custom_call_target="tpu_custom_call" | custom-call | tf_op jit(solution)/shard_map/pallas_call | solution.py:199
  35.6 1.7 %copy.5 = f32[3,128,8,256]{3,2,1,0:T(8,128)} copy(f32[3,128,8,256]{3,2,1,0:T(8,128)S(1)} %get-tuple-element.4) | data formatting | bytes 6291456
  37.3 1.7 %copy.6 = f32[3,128,8,256]{3,2,1,0:T(8,128)} copy(f32[3,128,8,256]{3,2,1,0:T(8,128)S(1)} %get-tuple-element.5) | data formatting | bytes 6291456
Async XLA Ops:
  0.6 1.9 %copy-start = (f32[3,128,8,256]{3,2,1,0:T(8,128)S(1)}, f32[3,128,8,256]{3,2,1,0:T(8,128)}, u32[]{:S(2)}) copy-start(f32[3,128,8,256]{3,2,1,0:T(8,128)} %vel.1) | copy-start | bytes 9437188

commit v2 on v1

--- a/solution.py
+++ b/solution.py
@@ -18,6 +18,7 @@
 WIDTH = 3
 CHUNKS = 8
 COMPS = 3
+PIECES = 4
 
 
 def kernel(
@@ -192,6 +193,24 @@
             copy.wait_send()
 
 
+def place_out(adv_in, gx_in, adv_out, gx_out, sem):
+    seg = adv_in.shape[1]
+    piece = seg // PIECES
+    copies = []
+    for part in range(PIECES):
+        planes = slice(part * piece, (part + 1) * piece)
+        for which, (source, target) in enumerate(((adv_in, adv_out), (gx_in, gx_out))):
+            copies.append(
+                pltpu.make_async_copy(
+                    source.at[:, planes], target.at[:, planes], sem.at[which, part]
+                )
+            )
+    for copy in copies:
+        copy.start()
+    for copy in copies:
+        copy.wait()
+
+
 def on_device(lines, tiles, velocity):
     comps, seg, rows, depth = velocity.shape
     plane = (comps, rows, depth)
@@ -199,7 +218,7 @@
     adv, gx = pl.pallas_call(
         functools.partial(kernel, lines, tiles),
         out_shape=(shape, shape),
-        in_specs=[pl.BlockSpec(memory_space=pl.ANY)],
+        in_specs=[pl.BlockSpec(memory_space=pltpu.HBM)],
         out_specs=(
             pl.BlockSpec(memory_space=pltpu.VMEM),
             pl.BlockSpec(memory_space=pltpu.VMEM),
@@ -219,10 +238,17 @@
             pltpu.SemaphoreType.DMA((2,)),
         ],
         compiler_params=pltpu.CompilerParams(
-            collective_id=0, has_side_effects=True, vmem_limit_bytes=40 * 1024 * 1024
+            collective_id=0, has_side_effects=True, vmem_limit_bytes=46 * 1024 * 1024
         ),
     )(velocity)
-    return adv, gx
+    return pl.pallas_call(
+        place_out,
+        out_shape=(shape, shape),
+        in_specs=[pl.BlockSpec(memory_space=pltpu.VMEM)] * 2,
+        out_specs=(pl.BlockSpec(memory_space=pltpu.HBM),) * 2,
+        scratch_shapes=[pltpu.SemaphoreType.DMA((2, PIECES))],
+        compiler_params=pltpu.CompilerParams(vmem_limit_bytes=24 * 1024 * 1024),
+    )(adv, gx)
 
 
 def solution(mesh):

time: 39.1 us -> 36.6 us (0.936)
  local copies, waits for them, and re-layouts: 5.21 us -> 0 us
  Pallas kernels: 33.1 us -> 35.8 us
    unnamed x4 -> x0, local copies, waits for them, and re-layouts: 5.21 us -> none
    pallas_call x0 -> x1, Pallas kernels: none -> 2.74 us  [on_device(): pl.pallas_call(place_out, out_shape=(shape, shape), in_specs=[pl.BlockSpe...]
where the time goes in v2:
time: 36.6 us; the launch traced here: 36.4 us
  Pallas kernels  35.8 us (98%)
  between operations  0.64 us (2%)
    pallas_call x1, Pallas kernels, on_device(): pl.pallas_call(functools.partial(kernel, lines, tiles), out_shape=(shape,...  33.1 us
    pallas_call x1, Pallas kernels, on_device(): pl.pallas_call(place_out, out_shape=(shape, shape), in_specs=[pl.BlockSpe...  2.74 us

profile of v2, /device:TPU:0, one launch (start us, length us, event | category | flops | bytes accessed | tf_op | source)
XLA Modules:
  0.0 36.4 jit_solution(1824897292173875892)
XLA Ops:
  0.6 33.1 %shard_map.30 = (f32[3,128,8,256]{3,2,1,0:T(8,128)S(1)}, f32[3,128,8,256]{3,2,1,0:T(8,128)S(1)}) custom-call(f32[3,128,8,256]{3,2,1,0:T(8,128)} %vel.1), custom_call_target="tpu_custom_call" | custom-call | tf_op jit(solution)/shard_map/pallas_call | solution.py:218
  33.7 2.7 %shard_map.31 = (f32[3,128,8,256]{3,2,1,0:T(8,128)}, f32[3,128,8,256]{3,2,1,0:T(8,128)}) custom-call(f32[3,128,8,256]{3,2,1,0:T(8,128)S(1)} %get-tuple-element.4.adv_in, f32[3,128,8,256]{3,2,1,0:T(8,128)S(1)} %get-tuple-element.5.gx_in), custom_call_target="tpu_custom_call" | custom-call | tf_op jit(solution)/shard_map/pallas_call | solution.py:244

commit v3 on v2

--- a/solution.py
+++ b/solution.py
@@ -16,7 +16,8 @@
 SCALE = 1.0 + ROOT * ROOT
 STENCIL = (45.0 / 60.0, -9.0 / 60.0, 1.0 / 60.0)
 WIDTH = 3
-CHUNKS = 8
+CHUNKS = 4
+CUTS = (0, 32, 56, 61, 64)
 COMPS = 3
 PIECES = 4
 
@@ -42,7 +43,7 @@
 ):
     seg = vel.shape[1]
     rows = vel.shape[2]
-    chunk = seg // CHUNKS
+    cuts = [seg * cut // CUTS[-1] for cut in CUTS]
     line = lax.axis_index("line")
     tile = lax.axis_index("cross")
     ahead = (lax.rem(line + 1, lines), tile)
@@ -77,7 +78,7 @@
 
     y_copies = []
     for part in range(CHUNKS):
-        planes = slice(part * chunk, (part + 1) * chunk)
+        planes = slice(cuts[part], cuts[part + 1])
         head = slice(0, WIDTH)
         tail = slice(rows - WIDTH, rows)
         pair = (
@@ -187,7 +188,7 @@
     for part in range(CHUNKS):
         for copy in y_copies[part]:
             copy.wait_recv()
-        lax.fori_loop(part * chunk, (part + 1) * chunk, along_y, 0, unroll=2)
+        lax.fori_loop(cuts[part], cuts[part + 1], along_y, 0, unroll=2)
     for pair in y_copies:
         for copy in pair:
             copy.wait_send()

time: 36.6 us -> 36.2 us (0.989)
  Pallas kernels: 35.8 us -> 35.4 us
    pallas_call x1, Pallas kernels: 33.1 us -> 32.7 us  [on_device(): pl.pallas_call(functools.partial(kernel, lines, tiles), out_shape=(shape,...]
where the time goes in v3:
time: 36.2 us; the launch traced here: 36.1 us
  Pallas kernels  35.4 us (98%)
  between operations  0.64 us (2%)
    pallas_call x1, Pallas kernels, on_device(): pl.pallas_call(functools.partial(kernel, lines, tiles), out_shape=(shape,...  32.7 us
    pallas_call x1, Pallas kernels, on_device(): pl.pallas_call(place_out, out_shape=(shape, shape), in_specs=[pl.BlockSpe...  2.74 us

profile of v3, /device:TPU:0, one launch (start us, length us, event | category | flops | bytes accessed | tf_op | source)
XLA Modules:
  0.0 36.1 jit_solution(18018400861380333818)
XLA Ops:
  0.6 32.7 %shard_map.30 = (f32[3,128,8,256]{3,2,1,0:T(8,128)S(1)}, f32[3,128,8,256]{3,2,1,0:T(8,128)S(1)}) custom-call(f32[3,128,8,256]{3,2,1,0:T(8,128)} %vel.1), custom_call_target="tpu_custom_call" | custom-call | tf_op jit(solution)/shard_map/pallas_call | solution.py:219
  33.3 2.7 %shard_map.31 = (f32[3,128,8,256]{3,2,1,0:T(8,128)}, f32[3,128,8,256]{3,2,1,0:T(8,128)}) custom-call(f32[3,128,8,256]{3,2,1,0:T(8,128)S(1)} %get-tuple-element.4.adv_in, f32[3,128,8,256]{3,2,1,0:T(8,128)S(1)} %get-tuple-element.5.gx_in), custom_call_target="tpu_custom_call" | custom-call | tf_op jit(solution)/shard_map/pallas_call | solution.py:245

commit v4 on v3

--- a/solution.py
+++ b/solution.py
@@ -17,7 +17,7 @@
 STENCIL = (45.0 / 60.0, -9.0 / 60.0, 1.0 / 60.0)
 WIDTH = 3
 CHUNKS = 4
-CUTS = (0, 32, 56, 61, 64)
+CUTS = (0, 28, 50, 60, 64)
 COMPS = 3
 PIECES = 4
 
@@ -97,9 +97,11 @@
                 below,
             ),
         )
-        for copy in pair:
-            copy.start()
         y_copies.append(pair)
+    around = (tile == tiles - 1, tile == 0)
+    for pair in y_copies:
+        for copy, wraps in zip(pair, around):
+            pl.when(wraps)(copy.start)
 
     def fill(i, value):
         power[i] = value
@@ -108,6 +110,9 @@
     lax.fori_loop(0, seg, fill, jnp.float32(ROOT))
 
     local.wait()
+    for pair in y_copies:
+        for copy, wraps in zip(pair, around):
+            pl.when(jnp.logical_not(wraps))(copy.start)
     for copy in x_copies:
         copy.wait()
 

time: 36.2 us -> 36.3 us (level)
  no operation moved by 1% of the time
where the time goes in v4:
time: 36.3 us; the launch traced here: 36.1 us
  Pallas kernels  35.5 us (98%)
  between operations  0.64 us (2%)
    pallas_call x1, Pallas kernels, on_device(): pl.pallas_call(functools.partial(kernel, lines, tiles), out_shape=(shape,...  32.7 us
    pallas_call x1, Pallas kernels, on_device(): pl.pallas_call(place_out, out_shape=(shape, shape), in_specs=[pl.BlockSpe...  2.74 us

profile of v4, /device:TPU:0, one launch (start us, length us, event | category | flops | bytes accessed | tf_op | source)
XLA Modules:
  0.0 36.1 jit_solution(4249460371530507745)
XLA Ops:
  0.6 32.7 %shard_map.30 = (f32[3,128,8,256]{3,2,1,0:T(8,128)S(1)}, f32[3,128,8,256]{3,2,1,0:T(8,128)S(1)}) custom-call(f32[3,128,8,256]{3,2,1,0:T(8,128)} %vel.1), custom_call_target="tpu_custom_call" | custom-call | tf_op jit(solution)/shard_map/pallas_call | solution.py:224
  33.4 2.7 %shard_map.31 = (f32[3,128,8,256]{3,2,1,0:T(8,128)}, f32[3,128,8,256]{3,2,1,0:T(8,128)}) custom-call(f32[3,128,8,256]{3,2,1,0:T(8,128)S(1)} %get-tuple-element.4.adv_in, f32[3,128,8,256]{3,2,1,0:T(8,128)S(1)} %get-tuple-element.5.gx_in), custom_call_target="tpu_custom_call" | custom-call | tf_op jit(solution)/shard_map/pallas_call | solution.py:250
